TPU v7x, 32 devices: a whole 2x2x4 slice. The times are simulated.
32 devices in a mesh: mem: 16 (over z, y, core), lon: 2 (over x).
Axes of the slice: x: 2, y: 2, z: 4, core: 2. Of those that a mesh axis runs over, the one named last changes fastest.
Arguments:
- ensemble: bfloat16 [32, 2, 256, 256], P('mem', None, None, 'lon'), may hold values from -6 to 6
- controls_start: float32 [32, 2, 256, 256], P('mem', None, None, 'lon'), may hold values from -6 to 6
- kappa_east: float32 [2, 256, 256], P(None, None, 'lon'), may hold values from 0.02 to 0.24
- kappa_north: float32 [2, 256, 256], P(None, None, 'lon'), may hold values from 0.02 to 0.24
- innovation: float32 [2, 256, 256], P(None, 'mem', 'lon'), may hold values from -6 to 6
- obs_mask: int32 [2, 256, 256], P(None, 'mem', 'lon'), may hold values 0 or 1
- gauge_index: int32 [2, 256, 256], P(None, 'mem', 'lon'), may hold values from 0 to 63
- gauge_precision: float32 [64], replicated, may hold values from 0.25 to 4
Outputs:
- controls: float32 [32, 2, 256, 256], P('mem', None, None, 'lon')
- increment: float32 [2, 256, 256], P(None, 'mem', 'lon')
All inputs are finite; a program needn't handle non-finite values. No bound on the sum of `obs_mask` on one device may be relied on, other than what follows from the above.
Results may differ from a plain program's by a relative error of at most 0.0003.
Values sent between devices are 32-bit elements; how exact they have to be, the bound alone decides.
A program may use at most 64 MiB of HBM per device.

v0:
```python
import functools

import jax
import jax.numpy as jnp
from jax import lax
from jax.experimental import pallas as pl
from jax.experimental.pallas import tpu as pltpu
from jax.sharding import PartitionSpec as P

STEPS = 6
ITERS = 2
SUBLANES = 8
LANES = 128
STEP_SIZE = 0.5
KAPPAS = ITERS
ENSEMBLE = ITERS + 1
FORCING = ITERS + 2
MESH = pl.DeviceIdType.MESH


def kernel(
    n_mem,
    n_lon,
    ens_ref,
    start_ref,
    east_ref,
    north_ref,
    innov_ref,
    mask_ref,
    gauge_ref,
    prec_ref,
    controls_ref,
    increment_ref,
    ctl,
    ens,
    work,
    east,
    north,
    forcing,
    partial,
    landing,
    edge_out,
    edge_in,
    plane,
    obs_out,
    obs_in,
    obs,
    own_inc,
    inc_out,
    inc_in,
    edge_send,
    edge_recv,
    sum_send,
    sum_recv,
    all_send,
    all_recv,
    obs_send,
    obs_recv,
    inc_send,
    inc_recv,
):
    members, levels, lat, lon = start_ref.shape
    gauges = prec_ref.shape[0]
    parts = SUBLANES // levels
    cols = lon // parts
    wide = cols + 2 * STEPS
    rows = 2 * SUBLANES
    own_cols = cols // n_mem
    chunk = own_cols * rows
    lat_block = lat // n_mem
    half_block = lat_block // 2
    packed = obs_out.shape[0] // n_mem
    scale = float(n_mem * members) ** (-0.5)
    me = lax.axis_index("mem")
    my_lon = lax.axis_index("lon")
    right = lax.rem(my_lon + 1, n_lon)
    left = lax.rem(my_lon + n_lon - 1, n_lon)
    lane = lax.broadcasted_iota(jnp.int32, (SUBLANES, LANES), 1)

    barrier = pltpu.get_barrier_semaphore()
    for off in range(1, n_mem):
        pl.semaphore_signal(barrier, inc=1, device_id={"mem": lax.rem(me + off, n_mem)}, device_id_type=MESH)
    for side in (left, right):
        pl.semaphore_signal(barrier, inc=1, device_id={"lon": side}, device_id_type=MESH)

    def at(k, parity, part, level):
        return k * rows + parity * SUBLANES + part * levels + level

    def enter(values, target, parity, level):
        turned = values.T
        for part in range(parts):
            target[pl.ds(at(STEPS, parity, part, level), cols, stride=rows), :] = turned[part * cols : (part + 1) * cols]

    def edge_copy(kind, way):
        return pltpu.make_async_remote_copy(
            src_ref=edge_out.at[kind, way],
            dst_ref=edge_in.at[kind, way],
            send_sem=edge_send.at[kind, way],
            recv_sem=edge_recv.at[kind, way],
            device_id={"lon": (right, left)[way]},
            device_id_type=MESH,
        )

    def slots(arrays):
        for index, array in enumerate(arrays):
            for parity in range(2):
                for level in range(levels):
                    yield (index * 2 + parity) * levels + level, array, parity, level

    def send_edges(kind, arrays):
        stride = len(arrays) * 2 * levels
        for q, array, parity, level in slots(arrays):
            edge_out[kind, 0, pl.ds(q, STEPS, stride=stride), :] = array[
                pl.ds(at(cols, parity, parts - 1, level), STEPS, stride=rows), :
            ]
            edge_out[kind, 1, pl.ds(q, STEPS, stride=stride), :] = array[
                pl.ds(at(STEPS, parity, 0, level), STEPS, stride=rows), :
            ]

    def start_edges(kind):
        for way in range(2):
            edge_copy(kind, way).start()

    def seams(arrays):
        for array in arrays:
            for k in range(STEPS):
                for parity in range(2):
                    here = at(k, parity, 0, 0)
                    there = at(cols + k, parity, 0, 0)
                    array[here : here + SUBLANES, :] = pltpu.roll(array[there : there + SUBLANES, :], levels, 0)
                    here = at(STEPS + cols + k, parity, 0, 0)
                    there = at(STEPS + k, parity, 0, 0)
                    array[here : here + SUBLANES, :] = pltpu.roll(
                        array[there : there + SUBLANES, :], SUBLANES - levels, 0
                    )

    def take_edges(kind, arrays):
        stride = len(arrays) * 2 * levels
        for way in range(2):
            edge_copy(kind, way).wait_recv()
        for q, array, parity, level in slots(arrays):
            array[pl.ds(at(0, parity, 0, level), STEPS, stride=rows), :] = edge_in[
                kind, 0, pl.ds(q, STEPS, stride=stride), :
            ]
            array[pl.ds(at(STEPS + cols, parity, parts - 1, level), STEPS, stride=rows), :] = edge_in[
                kind, 1, pl.ds(q, STEPS, stride=stride), :
            ]

    def column(k, count=1):
        return pl.ds(pl.multiple_of(k * rows, rows), count * rows)

    def diffuse(source):
        for section in range(1, STEPS + 1):
            now = source if section == 1 else work

            def advance(k, carry):
                coef_east = east[column(k), :]
                coef_north = north[column(k), :]
                result = []
                for member in range(members):
                    here, west_flux = carry[member]
                    ahead = now[member, column(k + 1), :]
                    flux = coef_east * (ahead - here)
                    even, odd = here[:SUBLANES], here[SUBLANES:]
                    even_flux = coef_north[:SUBLANES] * (odd - even)
                    odd_flux = coef_north[SUBLANES:] * (pltpu.roll(even, LANES - 1, 1) - odd)
                    base = here + (flux - west_flux)
                    work[member, column(k), :] = base + jnp.concatenate(
                        [even_flux - pltpu.roll(odd_flux, 1, 1), odd_flux - even_flux], axis=0
                    )
                    result.append((ahead, flux))
                return tuple(result)

            first = section
            begin = []
            for member in range(members):
                here = now[member, column(first), :]
                begin.append((here, east[column(first - 1), :] * (here - now[member, column(first - 1), :])))
            lax.fori_loop(first, wide - section, advance, tuple(begin), unroll=2)

    def spread(off, source, target, index, send, recv):
        return pltpu.make_async_remote_copy(
            src_ref=source,
            dst_ref=target,
            send_sem=send.at[index],
            recv_sem=recv.at[index],
            device_id={"mem": lax.rem(me + off, n_mem)},
            device_id_type=MESH,
        )

    def tile(index, size):
        return pl.ds(pl.multiple_of(index * size, size), size)

    def sum_copy(off):
        to = lax.rem(me + off, n_mem)
        return spread(off, partial.at[tile(to, chunk)], landing.at[off], off, sum_send, sum_recv)

    def all_copy(off, owner):
        block = forcing.at[pl.ds(pl.multiple_of(STEPS * rows + owner * chunk, rows), chunk)]
        return spread(off, block, block, off, all_send, all_recv)

    def obs_copy(off, owner):
        to = lax.rem(me + off, n_mem)
        return spread(off, obs_out.at[tile(to, packed)], obs_in.at[tile(owner, packed)], off, obs_send, obs_recv)

    def inc_copy(off, owner):
        to = lax.rem(me + off, n_mem)
        return spread(off, inc_out.at[tile(to, packed)], inc_in.at[tile(owner, packed)], off, inc_send, inc_recv)

    offsets = range(1, n_mem)

    def sender(off):
        return lax.rem(me + n_mem - off, n_mem)

    for member in range(members):
        for level in range(levels):
            for parity in range(2):
                enter(
                    start_ref[member, level, pl.ds(parity, LANES, stride=2), :], ctl.at[member], parity, level
                )
    controls = [ctl.at[member] for member in range(members)]
    send_edges(0, controls)
    pl.semaphore_wait(barrier, n_mem - 1 + 2)
    start_edges(0)

    for level in range(levels):
        for parity in range(2):
            enter(east_ref[level, pl.ds(parity, LANES, stride=2), :], east, parity, level)
            block = north_ref[level, pl.ds(parity, LANES, stride=2), :]
            if parity == 1:
                last = lax.broadcasted_iota(jnp.int32, block.shape, 0) == LANES - 1
                block = jnp.where(last, 0.0, block)
            enter(block, north, parity, level)
    send_edges(KAPPAS, [east, north])
    start_edges(KAPPAS)

    gauge = gauge_ref[...]

    def look_up(label, found):
        return jnp.where(gauge == label, prec_ref[label], found)

    precision = lax.fori_loop(0, gauges, look_up, jnp.zeros(gauge.shape, jnp.float32), unroll=8)
    weight = precision * mask_ref[...].astype(jnp.float32)
    plane[...] = jnp.zeros_like(plane)
    for level in range(levels):
        plane[LANES + level * lat_block : LANES + (level + 1) * lat_block, :] = weight[level]
    for parity in range(2):
        for level in range(levels):
            for q in range(2):
                start = ((q * 2 + parity) * levels + level) * half_block
                if q == 0:
                    values = plane[pl.ds(LANES + level * lat_block + parity, half_block, stride=2), :]
                else:
                    values = innov_ref[level, pl.ds(parity, half_block, stride=2), :]
                plane[start : start + half_block, :] = values
    plane[LANES:, :] = plane[:LANES, :].T
    for k in range(own_cols):
        for part in range(parts):
            obs_out[pl.ds(k * parts + part, n_mem, stride=packed), :] = plane[
                pl.ds(LANES + part * cols + k, n_mem, stride=own_cols), :
            ]
    for off in offsets:
        obs_copy(off, me).start()
    obs_in[tile(me, packed), :] = obs_out[tile(me, packed), :]

    for member in range(members):
        for level in range(levels):
            plane[...] = scale * ens_ref[member, level].astype(jnp.float32)
            for parity in range(2):
                enter(plane[pl.ds(parity, LANES, stride=2), :], ens.at[member], parity, level)
    members_of = [ens.at[member] for member in range(members)]
    send_edges(ENSEMBLE, members_of)
    start_edges(ENSEMBLE)

    seams(controls)
    seams([east, north])
    take_edges(0, controls)
    take_edges(KAPPAS, [east, north])

    for iteration in range(ITERS):
        diffuse(ctl)

        if iteration > 0:
            for off in offsets:
                sum_copy(off).wait_send()

        def add_members(k, unused):
            total = ens[0, column(k + STEPS), :] * work[0, column(k + STEPS), :]
            for member in range(1, members):
                total += ens[member, column(k + STEPS), :] * work[member, column(k + STEPS), :]
            partial[column(k), :] = total
            return unused

        lax.fori_loop(0, cols, add_members, 0, unroll=2)
        for off in offsets:
            sum_copy(off).start()

        if iteration == 0:
            seams(members_of)
            take_edges(ENSEMBLE, members_of)
            for off in offsets:
                obs_copy(off, sender(off)).wait_recv()
            for q in range(2):
                for parity in range(2):
                    for level in range(levels):
                        c = (q * 2 + parity) * levels + level
                        block = jnp.zeros((packed, LANES), jnp.float32)
                        for source in range(n_mem):
                            piece = obs_in[source * packed : (source + 1) * packed, :]
                            moved = pltpu.roll(piece, (source - c) * half_block % LANES, 1)
                            block = jnp.where(lane // half_block == source, moved, block)
                        for k in range(own_cols):
                            obs[q, pl.ds(at(k, parity, 0, level), parts, stride=levels), :] = block[
                                k * parts : (k + 1) * parts
                            ]

        total = partial[tile(me, chunk), :]
        for off in offsets:
            sum_copy(off).wait_recv()
            total += landing[off]
        own_inc[...] = total
        if iteration > 0:
            for off in offsets:
                all_copy(off, me).wait_send()
        forcing[pl.ds(pl.multiple_of(STEPS * rows + me * chunk, rows), chunk), :] = obs[0] * (total - obs[1])
        for off in offsets:
            all_copy(off, me).start()

        if iteration == ITERS - 1:
            plane[...] = jnp.zeros_like(plane)
            for parity in range(2):
                for level in range(levels):
                    for k in range(own_cols):
                        start = (parity * levels + level) * SUBLANES + k * parts
                        plane[start : start + parts, :] = own_inc[
                            pl.ds(at(k, parity, 0, level), parts, stride=levels), :
                        ]
            for target in range(n_mem):
                block = jnp.zeros((SUBLANES, LANES), jnp.float32)
                for c in range(2 * levels):
                    moved = pltpu.roll(
                        plane[c * SUBLANES : (c + 1) * SUBLANES, :], (c - target) * half_block % LANES, 1
                    )
                    block = jnp.where(lane // half_block == c, moved, block)
                inc_out[target * packed : (target + 1) * packed, :] = block
            for off in offsets:
                inc_copy(off, me).start()
            inc_in[tile(me, packed), :] = inc_out[tile(me, packed), :]

        for off in offsets:
            all_copy(off, sender(off)).wait_recv()
        send_edges(FORCING + iteration, [forcing])
        start_edges(FORCING + iteration)
        seams([forcing])
        take_edges(FORCING + iteration, [forcing])

        def force(k, unused):
            here = forcing[column(k), :]
            for member in range(members):
                work[member, column(k), :] = ens[member, column(k), :] * here
            return unused

        lax.fori_loop(0, wide, force, 0, unroll=2)
        diffuse(work)

        def update(k, unused):
            for member in range(members):
                before = ctl[member, column(k), :]
                ctl[member, column(k), :] = before - STEP_SIZE * (before + work[member, column(k), :])
            return unused

        lax.fori_loop(STEPS, STEPS + cols, update, 0, unroll=2)
        if iteration < ITERS - 1:
            send_edges(iteration + 1, controls)
            start_edges(iteration + 1)
            seams(controls)
            take_edges(iteration + 1, controls)

    for member in range(members):
        for level in range(levels):
            for parity in range(2):
                pieces = [
                    ctl[member, pl.ds(at(STEPS, parity, part, level), cols, stride=rows), :] for part in range(parts)
                ]
                controls_ref[member, level, pl.ds(parity, LANES, stride=2), :] = jnp.concatenate(pieces, axis=0).T

    for off in offsets:
        inc_copy(off, sender(off)).wait_recv()
    for k in range(own_cols):
        for part in range(parts):
            plane[pl.ds(part * cols + k, n_mem, stride=own_cols), :] = inc_in[
                pl.ds(k * parts + part, n_mem, stride=packed), :
            ]
    turned = plane[:LANES, :].T
    for parity in range(2):
        for level in range(levels):
            start = (parity * levels + level) * half_block
            increment_ref[level, pl.ds(parity, half_block, stride=2), :] = turned[start : start + half_block]

    for off in offsets:
        sum_copy(off).wait_send()
        all_copy(off, me).wait_send()
        obs_copy(off, me).wait_send()
        inc_copy(off, me).wait_send()
    for kind in range(FORCING + ITERS):
        for way in range(2):
            edge_copy(kind, way).wait_send()


def body(ensemble, controls_start, kappa_east, kappa_north, innovation, obs_mask, gauge_index, gauge_precision):
    n_mem, n_lon = lax.axis_size("mem"), lax.axis_size("lon")
    members, levels, lat, lon = controls_start.shape
    parts = SUBLANES // levels
    cols = lon // parts
    rows = 2 * SUBLANES
    wide = (cols + 2 * STEPS) * rows
    own_cols = cols // n_mem
    packed = -(-own_cols * parts // SUBLANES) * SUBLANES
    kinds = FORCING + ITERS
    edge = STEPS * max(members, 2) * 2 * levels

    def buffer(*shape):
        return pltpu.VMEM(shape + (LANES,), jnp.float32)

    pairs = [pltpu.SemaphoreType.DMA((kinds, 2))] * 2 + [pltpu.SemaphoreType.DMA((n_mem,))] * 8
    vmem = pl.BlockSpec(memory_space=pltpu.VMEM)
    flops = 4 * ITERS * STEPS * members * levels * lat * lon * 9
    return pl.pallas_call(
        functools.partial(kernel, n_mem, n_lon),
        out_shape=(
            jax.ShapeDtypeStruct(controls_start.shape, jnp.float32),
            jax.ShapeDtypeStruct(innovation.shape, jnp.float32),
        ),
        in_specs=[vmem] * 7 + [pl.BlockSpec(memory_space=pltpu.SMEM)],
        out_specs=(vmem, vmem),
        scratch_shapes=[
            buffer(members, wide),
            buffer(members, wide),
            buffer(members, wide),
            buffer(wide),
            buffer(wide),
            buffer(wide),
            buffer(cols * rows),
            buffer(n_mem, own_cols * rows),
            buffer(kinds, 2, edge),
            buffer(kinds, 2, edge),
            buffer(lat),
            buffer(n_mem * packed),
            buffer(n_mem * packed),
            buffer(2, own_cols * rows),
            buffer(own_cols * rows),
            buffer(n_mem * packed),
            buffer(n_mem * packed),
        ]
        + pairs,
        compiler_params=pltpu.CompilerParams(
            collective_id=0, has_side_effects=True, vmem_limit_bytes=32 * 1024 * 1024
        ),
        cost_estimate=pl.CostEstimate(flops=flops, bytes_accessed=2 * 1024 * 1024, transcendentals=0),
    )(ensemble, controls_start, kappa_east, kappa_north, innovation, obs_mask, gauge_index, gauge_precision)


def solution(mesh):
    in_specs = (
        P("mem", None, None, "lon"),
        P("mem", None, None, "lon"),
        P(None, None, "lon"),
        P(None, None, "lon"),
        P(None, "mem", "lon"),
        P(None, "mem", "lon"),
        P(None, "mem", "lon"),
        P(),
    )
    out_specs = (P("mem", None, None, "lon"), P(None, "mem", "lon"))
    return jax.shard_map(body, mesh=mesh, in_specs=in_specs, out_specs=out_specs, check_vma=False)
```

profile of v0, /device:TPU:0, one launch (start us, length us, event | category | flops | bytes accessed | tf_op | source)
XLA Modules:
  0.0 121.9 jit_solution(12410083862705992049)
XLA Ops:
  0.6 0.0 copy-start
  0.6 1.0 copy-done
  1.7 0.0 copy-start.1
  1.7 0.9 copy-done.1
  2.6 0.0 copy-start.2
  2.6 0.9 copy-done.2
  3.6 0.0 copy-start.3
  3.6 0.9 copy-done.3
  4.5 0.0 copy-start.4
  4.5 0.7 copy-done.4
  5.2 0.0 copy-start.5
  5.2 0.7 copy-done.5
  6.0 0.0 copy-start.6
  6.0 0.7 copy-done.6
  6.7 0.0 copy-start.7
  6.7 0.7 copy-done.7
  7.3 113.2 %shard_map.95 = (f32[2,2,256,128]{3,2,1,0:T(8,128)S(1)}, f32[2,16,128]{2,1,0:T(8,128)S(1)}) custom-call(bf16[2,2,256,128]{3,2,1,0:T(8,128)(2,1)S(1)} %copy-done.1, f32[2,2,256,128]{3,2,1,0:T(8,128)S(1)} %copy-done, f32[2,256,128]{2,1,0:T(8,128)S(1)} %copy-done.2, f32[2,256,128]{2,1,0:T(8,128)S(1)} %copy-done.3, f32[2,16,128]{2,1,0:T(8,128)S(1)} %copy-done.4, ...), custom_call_target="tpu_custom_call" | custom-call | flops 56623104 | bytes 2097152 | tf_op jit(solution)/shard_map/pallas_call | solution.py:428
  120.5 0.8 copy.12
  121.3 0.6 copy.13
Async XLA Ops:
  0.6 1.0 copy-start
  1.7 0.9 copy-start.1
  2.6 0.9 copy-start.2
  3.6 0.9 copy-start.3
  4.5 0.7 copy-start.4
  5.2 0.7 copy-start.5
  6.0 0.7 copy-start.6
  6.7 0.7 copy-start.7
where the time goes:
time: 122 us
  Pallas kernels  113 us (93%)
  local copies, waits for them, and re-layouts  8.09 us (7%)
    pallas_call x1, Pallas kernels, body(): pl.pallas_call(functools.partial(kernel, n_mem, n_lon), out_shape=(jax.Sh...  113 us
    unnamed x18, local copies, waits for them, and re-layouts  8.09 us

commit v1 on v0

--- a/solution.py
+++ b/solution.py
@@ -21,13 +21,13 @@
 def kernel(
     n_mem,
     n_lon,
-    ens_ref,
-    start_ref,
-    east_ref,
-    north_ref,
-    innov_ref,
-    mask_ref,
-    gauge_ref,
+    ens_hbm,
+    start_hbm,
+    east_hbm,
+    north_hbm,
+    innov_hbm,
+    mask_hbm,
+    gauge_hbm,
     prec_ref,
     controls_ref,
     increment_ref,
@@ -48,6 +48,14 @@
     own_inc,
     inc_out,
     inc_in,
+    start_ref,
+    east_ref,
+    north_ref,
+    gauge_ref,
+    mask_ref,
+    innov_ref,
+    ens_ref,
+    fetch_sem,
     edge_send,
     edge_recv,
     sum_send,
@@ -77,6 +85,23 @@
     left = lax.rem(my_lon + n_lon - 1, n_lon)
     lane = lax.broadcasted_iota(jnp.int32, (SUBLANES, LANES), 1)
 
+    fetches = [
+        pltpu.make_async_copy(source, target, fetch_sem.at[index])
+        for index, (source, target) in enumerate(
+            (
+                (start_hbm, start_ref),
+                (east_hbm, east_ref),
+                (north_hbm, north_ref),
+                (gauge_hbm, gauge_ref),
+                (mask_hbm, mask_ref),
+                (innov_hbm, innov_ref),
+                (ens_hbm, ens_ref),
+            )
+        )
+    ]
+    for fetch in fetches:
+        fetch.start()
+
     barrier = pltpu.get_barrier_semaphore()
     for off in range(1, n_mem):
         pl.semaphore_signal(barrier, inc=1, device_id={"mem": lax.rem(me + off, n_mem)}, device_id_type=MESH)
@@ -146,37 +171,70 @@
                 kind, 1, pl.ds(q, STEPS, stride=stride), :
             ]
 
-    def column(k, count=1):
-        return pl.ds(pl.multiple_of(k * rows, rows), count * rows)
-
-    def diffuse(source):
-        for section in range(1, STEPS + 1):
-            now = source if section == 1 else work
-
-            def advance(k, carry):
-                coef_east = east[column(k), :]
-                coef_north = north[column(k), :]
-                result = []
-                for member in range(members):
-                    here, west_flux = carry[member]
-                    ahead = now[member, column(k + 1), :]
-                    flux = coef_east * (ahead - here)
-                    even, odd = here[:SUBLANES], here[SUBLANES:]
-                    even_flux = coef_north[:SUBLANES] * (odd - even)
-                    odd_flux = coef_north[SUBLANES:] * (pltpu.roll(even, LANES - 1, 1) - odd)
-                    base = here + (flux - west_flux)
-                    work[member, column(k), :] = base + jnp.concatenate(
-                        [even_flux - pltpu.roll(odd_flux, 1, 1), odd_flux - even_flux], axis=0
-                    )
-                    result.append((ahead, flux))
-                return tuple(result)
-
-            first = section
-            begin = []
+    def step(first, last, span, load, store):
+        behind = []
+        current = []
+        for member in range(members):
+            pair = load(member, first - 1, 2)
+            old, here = pair[:rows], pair[rows:]
+            behind.append(east[(first - 1) * rows : first * rows, :] * (here - old))
+            current.append(here)
+        for k in range(first, last, span):
+            lanes = slice(k * rows, (k + span) * rows)
+            coef_east = east[lanes, :]
+            coef_north = north[lanes, :].reshape(span, 2, SUBLANES, LANES)
+            results = []
             for member in range(members):
-                here = now[member, column(first), :]
-                begin.append((here, east[column(first - 1), :] * (here - now[member, column(first - 1), :])))
-            lax.fori_loop(first, wide - section, advance, tuple(begin), unroll=2)
+                after = load(member, k + 1, span)
+                here = jnp.concatenate([current[member], after[: (span - 1) * rows]], axis=0)
+                flux = coef_east * (after - here)
+                west = jnp.concatenate([behind[member], flux[: (span - 1) * rows]], axis=0)
+                pairs = here.reshape(span, 2, SUBLANES, LANES)
+                even, odd = pairs[:, 0], pairs[:, 1]
+                even_flux = coef_north[:, 0] * (odd - even)
+                odd_flux = coef_north[:, 1] * (pltpu.roll(even, LANES - 1, 2) - odd)
+                change = jnp.stack([even_flux - pltpu.roll(odd_flux, 1, 2), odd_flux - even_flux], axis=1)
+                results.append(here + (flux - west) + change.reshape(span * rows, LANES))
+                current[member] = after[(span - 1) * rows :]
+                behind[member] = flux[(span - 1) * rows :]
+            store(k, span, results)
+
+    def load_work(member, k, count):
+        return work[member, k * rows : (k + count) * rows, :]
+
+    def store_work(k, count, results):
+        for member in range(members):
+            work[member, k * rows : (k + count) * rows, :] = results[member]
+
+    def diffuse(load, store):
+        step(1, wide - 1, 6, load, store_work)
+
+        def middle(section, unused):
+            step(2, wide - 2, 4, load_work, store_work)
+            return unused
+
+        lax.fori_loop(0, STEPS - 2, middle, 0)
+        step(STEPS, STEPS + cols, 4, load_work, store)
+
+    def load_controls(member, k, count):
+        return ctl[member, k * rows : (k + count) * rows, :]
+
+    def store_sum(k, count, results):
+        span = slice(k * rows, (k + count) * rows)
+        total = ens[0, span, :] * results[0]
+        for member in range(1, members):
+            total += ens[member, span, :] * results[member]
+        partial[(k - STEPS) * rows : (k - STEPS + count) * rows, :] = total
+
+    def load_forced(member, k, count):
+        span = slice(k * rows, (k + count) * rows)
+        return ens[member, span, :] * forcing[span, :]
+
+    def store_update(k, count, results):
+        span = slice(k * rows, (k + count) * rows)
+        for member in range(members):
+            before = ctl[member, span, :]
+            ctl[member, span, :] = before - STEP_SIZE * (before + results[member])
 
     def spread(off, source, target, index, send, recv):
         return pltpu.make_async_remote_copy(
@@ -212,6 +270,7 @@
     def sender(off):
         return lax.rem(me + n_mem - off, n_mem)
 
+    fetches[0].wait()
     for member in range(members):
         for level in range(levels):
             for parity in range(2):
@@ -223,6 +282,8 @@
     pl.semaphore_wait(barrier, n_mem - 1 + 2)
     start_edges(0)
 
+    fetches[1].wait()
+    fetches[2].wait()
     for level in range(levels):
         for parity in range(2):
             enter(east_ref[level, pl.ds(parity, LANES, stride=2), :], east, parity, level)
@@ -234,6 +295,8 @@
     send_edges(KAPPAS, [east, north])
     start_edges(KAPPAS)
 
+    for index in (3, 4, 5):
+        fetches[index].wait()
     gauge = gauge_ref[...]
 
     def look_up(label, found):
@@ -263,6 +326,7 @@
         obs_copy(off, me).start()
     obs_in[tile(me, packed), :] = obs_out[tile(me, packed), :]
 
+    fetches[6].wait()
     for member in range(members):
         for level in range(levels):
             plane[...] = scale * ens_ref[member, level].astype(jnp.float32)
@@ -278,20 +342,10 @@
     take_edges(KAPPAS, [east, north])
 
     for iteration in range(ITERS):
-        diffuse(ctl)
-
         if iteration > 0:
             for off in offsets:
                 sum_copy(off).wait_send()
-
-        def add_members(k, unused):
-            total = ens[0, column(k + STEPS), :] * work[0, column(k + STEPS), :]
-            for member in range(1, members):
-                total += ens[member, column(k + STEPS), :] * work[member, column(k + STEPS), :]
-            partial[column(k), :] = total
-            return unused
-
-        lax.fori_loop(0, cols, add_members, 0, unroll=2)
+        diffuse(load_controls, store_sum)
         for off in offsets:
             sum_copy(off).start()
 
@@ -354,22 +408,7 @@
         seams([forcing])
         take_edges(FORCING + iteration, [forcing])
 
-        def force(k, unused):
-            here = forcing[column(k), :]
-            for member in range(members):
-                work[member, column(k), :] = ens[member, column(k), :] * here
-            return unused
-
-        lax.fori_loop(0, wide, force, 0, unroll=2)
-        diffuse(work)
-
-        def update(k, unused):
-            for member in range(members):
-                before = ctl[member, column(k), :]
-                ctl[member, column(k), :] = before - STEP_SIZE * (before + work[member, column(k), :])
-            return unused
-
-        lax.fori_loop(STEPS, STEPS + cols, update, 0, unroll=2)
+        diffuse(load_forced, store_update)
         if iteration < ITERS - 1:
             send_edges(iteration + 1, controls)
             start_edges(iteration + 1)
@@ -431,7 +470,7 @@
             jax.ShapeDtypeStruct(controls_start.shape, jnp.float32),
             jax.ShapeDtypeStruct(innovation.shape, jnp.float32),
         ),
-        in_specs=[vmem] * 7 + [pl.BlockSpec(memory_space=pltpu.SMEM)],
+        in_specs=[pl.BlockSpec(memory_space=pltpu.HBM)] * 7 + [pl.BlockSpec(memory_space=pltpu.SMEM)],
         out_specs=(vmem, vmem),
         scratch_shapes=[
             buffer(members, wide),
@@ -451,6 +490,14 @@
             buffer(own_cols * rows),
             buffer(n_mem * packed),
             buffer(n_mem * packed),
+            pltpu.VMEM(controls_start.shape, jnp.float32),
+            pltpu.VMEM(kappa_east.shape, jnp.float32),
+            pltpu.VMEM(kappa_north.shape, jnp.float32),
+            pltpu.VMEM(gauge_index.shape, jnp.int32),
+            pltpu.VMEM(obs_mask.shape, jnp.int32),
+            pltpu.VMEM(innovation.shape, jnp.float32),
+            pltpu.VMEM(ensemble.shape, ensemble.dtype),
+            pltpu.SemaphoreType.DMA((7,)),
         ]
         + pairs,
         compiler_params=pltpu.CompilerParams(

time: 122 us -> 67.7 us (0.55)
  Pallas kernels: 113 us -> 58.5 us
    pallas_call x1, Pallas kernels: 113 us -> 58.5 us  [body(): pl.pallas_call(functools.partial(kernel, n_mem, n_lon), out_shape=(jax.Sh...]
where the time goes in v1:
time: 67.7 us; the launch traced here: 67.2 us
  Pallas kernels  58.5 us (86%)
  local copies, waits for them, and re-layouts  8.09 us (12%)
    pallas_call x1, Pallas kernels, body(): pl.pallas_call(functools.partial(kernel, n_mem, n_lon), out_shape=(jax.Sh...  58.5 us
    unnamed x18, local copies, waits for them, and re-layouts  8.09 us

profile of v1, /device:TPU:0, one launch (start us, length us, event | category | flops | bytes accessed | tf_op | source)
XLA Modules:
  0.0 67.2 jit_solution(1595576437101125607)
XLA Ops:
  0.6 0.0 copy-start
  0.6 1.0 %copy-done = f32[2,2,256,128]{3,2,1,0:T(8,128)S(1)} copy-done((f32[2,2,256,128]{3,2,1,0:T(8,128)S(1)}, f32[2,2,256,128]{3,2,1,0:T(8,128)}, u32[]{:S(2)}) %copy-start) | copy-done | bytes 524312
  1.7 0.0 copy-start.1
  1.7 0.9 %copy-done.1 = bf16[2,2,256,128]{3,2,1,0:T(8,128)(2,1)S(1)} copy-done((bf16[2,2,256,128]{3,2,1,0:T(8,128)(2,1)S(1)}, bf16[2,2,256,128]{3,2,1,0:T(8,128)(2,1)}, u32[]{:S(2)}) %copy-start.1) | copy-done | bytes 262168
  2.6 0.0 copy-start.2
  2.6 0.9 %copy-done.2 = f32[2,256,128]{2,1,0:T(8,128)S(1)} copy-done((f32[2,256,128]{2,1,0:T(8,128)S(1)}, f32[2,256,128]{2,1,0:T(8,128)}, u32[]{:S(2)}) %copy-start.2) | copy-done | bytes 262168
  3.6 0.0 copy-start.3
  3.6 0.9 %copy-done.3 = f32[2,256,128]{2,1,0:T(8,128)S(1)} copy-done((f32[2,256,128]{2,1,0:T(8,128)S(1)}, f32[2,256,128]{2,1,0:T(8,128)}, u32[]{:S(2)}) %copy-start.3) | copy-done | bytes 262168
  4.5 0.0 copy-start.4
  4.5 0.7 %copy-done.4 = f32[2,16,128]{2,1,0:T(8,128)S(1)} copy-done((f32[2,16,128]{2,1,0:T(8,128)S(1)}, f32[2,16,128]{2,1,0:T(8,128)}, u32[]{:S(2)}) %copy-start.4) | copy-done | bytes 16408
  5.2 0.0 copy-start.5
  5.2 0.7 %copy-done.5 = s32[2,16,128]{2,1,0:T(8,128)S(1)} copy-done((s32[2,16,128]{2,1,0:T(8,128)S(1)}, s32[2,16,128]{2,1,0:T(8,128)}, u32[]{:S(2)}) %copy-start.5) | copy-done | bytes 16408
  6.0 0.0 copy-start.6
  6.0 0.7 %copy-done.6 = s32[2,16,128]{2,1,0:T(8,128)S(1)} copy-done((s32[2,16,128]{2,1,0:T(8,128)S(1)}, s32[2,16,128]{2,1,0:T(8,128)}, u32[]{:S(2)}) %copy-start.6) | copy-done | bytes 16408
  6.7 0.0 copy-start.7
  6.7 0.7 copy-done.7
  7.3 58.5 %shard_map.95 = (f32[2,2,256,128]{3,2,1,0:T(8,128)S(1)}, f32[2,16,128]{2,1,0:T(8,128)S(1)}) custom-call(bf16[2,2,256,128]{3,2,1,0:T(8,128)(2,1)S(1)} %copy-done.1, f32[2,2,256,128]{3,2,1,0:T(8,128)S(1)} %copy-done, f32[2,256,128]{2,1,0:T(8,128)S(1)} %copy-done.2, f32[2,256,128]{2,1,0:T(8,128)S(1)} %copy-done.3, f32[2,16,128]{2,1,0:T(8,128)S(1)} %copy-done.4, ...), custom_call_target="tpu_custom_call" | custom-call | flops 56623104 | bytes 2097152 | tf_op jit(solution)/shard_map/pallas_call | solution.py:467
  65.8 0.8 %copy.12 = f32[2,2,256,128]{3,2,1,0:T(8,128)} copy(f32[2,2,256,128]{3,2,1,0:T(8,128)S(1)} %get-tuple-element.4) | data formatting | bytes 1048576
  66.6 0.6 copy.13
Async XLA Ops:
  0.6 1.0 %copy-start = (f32[2,2,256,128]{3,2,1,0:T(8,128)S(1)}, f32[2,2,256,128]{3,2,1,0:T(8,128)}, u32[]{:S(2)}) copy-start(f32[2,2,256,128]{3,2,1,0:T(8,128)} %start_hbm.1) | copy-start | bytes 1572868
  1.7 0.9 %copy-start.1 = (bf16[2,2,256,128]{3,2,1,0:T(8,128)(2,1)S(1)}, bf16[2,2,256,128]{3,2,1,0:T(8,128)(2,1)}, u32[]{:S(2)}) copy-start(bf16[2,2,256,128]{3,2,1,0:T(8,128)(2,1)} %ens_hbm.1) | copy-start | bytes 786436
  2.6 0.9 %copy-start.2 = (f32[2,256,128]{2,1,0:T(8,128)S(1)}, f32[2,256,128]{2,1,0:T(8,128)}, u32[]{:S(2)}) copy-start(f32[2,256,128]{2,1,0:T(8,128)} %east_hbm.1) | copy-start | bytes 786436
  3.6 0.9 %copy-start.3 = (f32[2,256,128]{2,1,0:T(8,128)S(1)}, f32[2,256,128]{2,1,0:T(8,128)}, u32[]{:S(2)}) copy-start(f32[2,256,128]{2,1,0:T(8,128)} %north_hbm.1) | copy-start | bytes 786436
  4.5 0.7 %copy-start.4 = (f32[2,16,128]{2,1,0:T(8,128)S(1)}, f32[2,16,128]{2,1,0:T(8,128)}, u32[]{:S(2)}) copy-start(f32[2,16,128]{2,1,0:T(8,128)} %innov_hbm.1) | copy-start | bytes 49156
  5.2 0.7 %copy-start.5 = (s32[2,16,128]{2,1,0:T(8,128)S(1)}, s32[2,16,128]{2,1,0:T(8,128)}, u32[]{:S(2)}) copy-start(s32[2,16,128]{2,1,0:T(8,128)} %mask_hbm.1) | copy-start | bytes 49156
  6.0 0.7 %copy-start.6 = (s32[2,16,128]{2,1,0:T(8,128)S(1)}, s32[2,16,128]{2,1,0:T(8,128)}, u32[]{:S(2)}) copy-start(s32[2,16,128]{2,1,0:T(8,128)} %gauge_hbm.1) | copy-start | bytes 49156
  6.7 0.7 copy-start.7

commit v2 on v1

--- a/solution.py
+++ b/solution.py
@@ -38,6 +38,7 @@
     north,
     forcing,
     partial,
+    pair_in,
     landing,
     edge_out,
     edge_in,
@@ -58,10 +59,14 @@
     fetch_sem,
     edge_send,
     edge_recv,
+    pair_send,
+    pair_recv,
     sum_send,
     sum_recv,
     all_send,
     all_recv,
+    pass_send,
+    pass_recv,
     obs_send,
     obs_recv,
     inc_send,
@@ -236,39 +241,64 @@
             before = ctl[member, span, :]
             ctl[member, span, :] = before - STEP_SIZE * (before + results[member])
 
-    def spread(off, source, target, index, send, recv):
+    def tile(index, size):
+        return pl.ds(pl.multiple_of(index * size, size), size)
+
+    def send(source, target, send_sem, recv_sem, to):
         return pltpu.make_async_remote_copy(
             src_ref=source,
             dst_ref=target,
-            send_sem=send.at[index],
-            recv_sem=recv.at[index],
-            device_id={"mem": lax.rem(me + off, n_mem)},
+            send_sem=send_sem,
+            recv_sem=recv_sem,
+            device_id={"mem": to},
             device_id_type=MESH,
         )
 
-    def tile(index, size):
-        return pl.ds(pl.multiple_of(index * size, size), size)
-
-    def sum_copy(off):
-        to = lax.rem(me + off, n_mem)
-        return spread(off, partial.at[tile(to, chunk)], landing.at[off], off, sum_send, sum_recv)
-
-    def all_copy(off, owner):
-        block = forcing.at[pl.ds(pl.multiple_of(STEPS * rows + owner * chunk, rows), chunk)]
-        return spread(off, block, block, off, all_send, all_recv)
+    pairs = n_mem // 2
+    core = lax.rem(me, 2)
+    group = lax.div(me, 2)
+    sibling = me + 1 - 2 * core
+    offsets = range(1, n_mem)
+    hops = range(1, pairs)
+
+    mine = core * pairs + group
+
+    def chunk_of(device):
+        return lax.rem(device, 2) * pairs + lax.div(device, 2)
+
+    def sender(off):
+        return lax.rem(me + n_mem - off, n_mem)
+
+    def pair_copy():
+        half = pairs * chunk
+        return send(partial.at[tile(1 - core, half)], pair_in, pair_send.at[0], pair_recv.at[0], sibling)
+
+    def sum_copy(hop):
+        to = lax.rem(group + hop, pairs)
+        source = partial.at[tile(core * pairs + to, chunk)]
+        return send(source, landing.at[hop], sum_send.at[hop], sum_recv.at[hop], to * 2 + core)
+
+    def block_of(index):
+        return pl.ds(pl.multiple_of(STEPS * rows + index * chunk, rows), chunk)
+
+    def all_copy(hop, index):
+        block = forcing.at[block_of(index)]
+        to = lax.rem(group + hop, pairs) * 2 + core
+        return send(block, block, all_send.at[hop], all_recv.at[hop], to)
+
+    def pass_copy(hop, side):
+        block = forcing.at[block_of(side * pairs + lax.rem(group + pairs - hop, pairs))]
+        return send(block, block, pass_send.at[hop], pass_recv.at[hop], sibling)
 
     def obs_copy(off, owner):
         to = lax.rem(me + off, n_mem)
-        return spread(off, obs_out.at[tile(to, packed)], obs_in.at[tile(owner, packed)], off, obs_send, obs_recv)
+        source = obs_out.at[tile(chunk_of(to), packed)]
+        return send(source, obs_in.at[tile(owner, packed)], obs_send.at[off], obs_recv.at[off], to)
 
     def inc_copy(off, owner):
         to = lax.rem(me + off, n_mem)
-        return spread(off, inc_out.at[tile(to, packed)], inc_in.at[tile(owner, packed)], off, inc_send, inc_recv)
-
-    offsets = range(1, n_mem)
-
-    def sender(off):
-        return lax.rem(me + n_mem - off, n_mem)
+        target = inc_in.at[tile(chunk_of(owner), packed)]
+        return send(inc_out.at[tile(to, packed)], target, inc_send.at[off], inc_recv.at[off], to)
 
     fetches[0].wait()
     for member in range(members):
@@ -324,7 +354,7 @@
             ]
     for off in offsets:
         obs_copy(off, me).start()
-    obs_in[tile(me, packed), :] = obs_out[tile(me, packed), :]
+    obs_in[tile(me, packed), :] = obs_out[tile(chunk_of(me), packed), :]
 
     fetches[6].wait()
     for member in range(members):
@@ -343,12 +373,21 @@
 
     for iteration in range(ITERS):
         if iteration > 0:
-            for off in offsets:
-                sum_copy(off).wait_send()
+            pair_copy().wait_send()
+            for hop in hops:
+                sum_copy(hop).wait_send()
+                all_copy(hop, mine).wait_send()
+            for hop in range(pairs):
+                pass_copy(hop, core).wait_send()
         diffuse(load_controls, store_sum)
-        for off in offsets:
-            sum_copy(off).start()
-
+        pair_copy().start()
+
+        pair_copy().wait_recv()
+        for hop in hops:
+            to = lax.rem(group + hop, pairs)
+            partial[tile(core * pairs + to, chunk), :] += pair_in[tile(to, chunk), :]
+            sum_copy(hop).start()
+        total = partial[tile(mine, chunk), :] + pair_in[tile(group, chunk), :]
         if iteration == 0:
             seams(members_of)
             take_edges(ENSEMBLE, members_of)
@@ -367,18 +406,23 @@
                             obs[q, pl.ds(at(k, parity, 0, level), parts, stride=levels), :] = block[
                                 k * parts : (k + 1) * parts
                             ]
-
-        total = partial[tile(me, chunk), :]
-        for off in offsets:
-            sum_copy(off).wait_recv()
-            total += landing[off]
+        for hop in hops:
+            sum_copy(hop).wait_recv()
+            total += landing[hop]
         own_inc[...] = total
-        if iteration > 0:
-            for off in offsets:
-                all_copy(off, me).wait_send()
-        forcing[pl.ds(pl.multiple_of(STEPS * rows + me * chunk, rows), chunk), :] = obs[0] * (total - obs[1])
-        for off in offsets:
-            all_copy(off, me).start()
+        forcing[block_of(mine), :] = obs[0] * (total - obs[1])
+        for hop in hops:
+            all_copy(hop, mine).start()
+        pass_copy(0, core).start()
+
+        for hop in hops:
+            all_copy(hop, core * pairs + lax.rem(group + pairs - hop, pairs)).wait_recv()
+            pass_copy(hop, core).start()
+        for hop in range(pairs):
+            pass_copy(hop, 1 - core).wait_recv()
+        send_edges(FORCING + iteration, [forcing])
+        start_edges(FORCING + iteration)
+        seams([forcing])
 
         if iteration == ITERS - 1:
             plane[...] = jnp.zeros_like(plane)
@@ -399,13 +443,8 @@
                 inc_out[target * packed : (target + 1) * packed, :] = block
             for off in offsets:
                 inc_copy(off, me).start()
-            inc_in[tile(me, packed), :] = inc_out[tile(me, packed), :]
-
-        for off in offsets:
-            all_copy(off, sender(off)).wait_recv()
-        send_edges(FORCING + iteration, [forcing])
-        start_edges(FORCING + iteration)
-        seams([forcing])
+            inc_in[tile(chunk_of(me), packed), :] = inc_out[tile(me, packed), :]
+
         take_edges(FORCING + iteration, [forcing])
 
         diffuse(load_forced, store_update)
@@ -436,9 +475,13 @@
             start = (parity * levels + level) * half_block
             increment_ref[level, pl.ds(parity, half_block, stride=2), :] = turned[start : start + half_block]
 
+    pair_copy().wait_send()
+    for hop in hops:
+        sum_copy(hop).wait_send()
+        all_copy(hop, mine).wait_send()
+    for hop in range(pairs):
+        pass_copy(hop, core).wait_send()
     for off in offsets:
-        sum_copy(off).wait_send()
-        all_copy(off, me).wait_send()
         obs_copy(off, me).wait_send()
         inc_copy(off, me).wait_send()
     for kind in range(FORCING + ITERS):
@@ -461,7 +504,7 @@
     def buffer(*shape):
         return pltpu.VMEM(shape + (LANES,), jnp.float32)
 
-    pairs = [pltpu.SemaphoreType.DMA((kinds, 2))] * 2 + [pltpu.SemaphoreType.DMA((n_mem,))] * 8
+    pairs = [pltpu.SemaphoreType.DMA((kinds, 2))] * 2 + [pltpu.SemaphoreType.DMA((n_mem,))] * 12
     vmem = pl.BlockSpec(memory_space=pltpu.VMEM)
     flops = 4 * ITERS * STEPS * members * levels * lat * lon * 9
     return pl.pallas_call(
@@ -480,7 +523,8 @@
             buffer(wide),
             buffer(wide),
             buffer(cols * rows),
-            buffer(n_mem, own_cols * rows),
+            buffer(n_mem // 2 * own_cols * rows),
+            buffer(n_mem // 2, own_cols * rows),
             buffer(kinds, 2, edge),
             buffer(kinds, 2, edge),
             buffer(lat),
@@ -501,7 +545,7 @@
         ]
         + pairs,
         compiler_params=pltpu.CompilerParams(
-            collective_id=0, has_side_effects=True, vmem_limit_bytes=32 * 1024 * 1024
+            collective_id=0, has_side_effects=True, vmem_limit_bytes=60 * 1024 * 1024
         ),
         cost_estimate=pl.CostEstimate(flops=flops, bytes_accessed=2 * 1024 * 1024, transcendentals=0),
     )(ensemble, controls_start, kappa_east, kappa_north, innovation, obs_mask, gauge_index, gauge_precision)

time: 67.7 us -> 58.9 us (0.87)
  local copies, waits for them, and re-layouts: 8.09 us -> 2.48 us
  Pallas kernels: 58.5 us -> 55.3 us
    unnamed x18 -> x4, local copies, waits for them, and re-layouts: 8.09 us -> 2.48 us
    pallas_call x1, Pallas kernels: 58.5 us -> 55.3 us  [body(): pl.pallas_call(functools.partial(kernel, n_mem, n_lon), out_shape=(jax.Sh...]
where the time goes in v2:
time: 58.9 us; the launch traced here: 58.4 us
  Pallas kernels  55.3 us (94%)
  local copies, waits for them, and re-layouts  2.48 us (4%)
  between operations  0.65 us (1%)
    pallas_call x1, Pallas kernels, body(): pl.pallas_call(functools.partial(kernel, n_mem, n_lon), out_shape=(jax.Sh...  55.3 us
    unnamed x4, local copies, waits for them, and re-layouts  2.48 us

profile of v2, /device:TPU:0, one launch (start us, length us, event | category | flops | bytes accessed | tf_op | source)
XLA Modules:
  0.0 58.4 jit_solution(4586990233873918934)
XLA Ops:
  0.6 55.3 %shard_map.95 = (f32[2,2,256,128]{3,2,1,0:T(8,128)}, f32[2,16,128]{2,1,0:T(8,128)}) custom-call(bf16[2,2,256,128]{3,2,1,0:T(8,128)(2,1)} %ens_hbm.1, f32[2,2,256,128]{3,2,1,0:T(8,128)} %start_hbm.1, f32[2,256,128]{2,1,0:T(8,128)} %east_hbm.1, f32[2,256,128]{2,1,0:T(8,128)} %north_hbm.1, f32[2,16,128]{2,1,0:T(8,128)} %innov_hbm.1, s32[2,16,128]{2,1,0:T(8,128)} %mask_hbm.1, ...), custom_call_target="tpu_custom_call" | custom-call | flops 56623104 | bytes 2097152 | tf_op jit(solution)/shard_map/pallas_call | solution.py:510
  55.9 0.0 copy-start
  56.0 1.9 %copy.12 = f32[2,2,256,128]{3,2,1,0:T(8,128)} copy(f32[2,2,256,128]{3,2,1,0:T(8,128)} %get-tuple-element.4) | data formatting | bytes 1048576
  57.8 0.0 copy-done
  57.8 0.6 %copy.13 = f32[2,16,128]{2,1,0:T(8,128)} copy(f32[2,16,128]{2,1,0:T(8,128)S(1)} %copy-done) | data formatting | bytes 32768
Async XLA Ops:
  55.9 1.9 %copy-start = (f32[2,16,128]{2,1,0:T(8,128)S(1)}, f32[2,16,128]{2,1,0:T(8,128)}, u32[]{:S(2)}) copy-start(f32[2,16,128]{2,1,0:T(8,128)} %get-tuple-element.5) | copy-start | bytes 49156

commit v3 on v2

--- a/solution.py
+++ b/solution.py
@@ -9,6 +9,7 @@
 
 STEPS = 6
 ITERS = 2
+SPAN = 6
 SUBLANES = 8
 LANES = 128
 STEP_SIZE = 0.5
@@ -36,6 +37,7 @@
     work,
     east,
     north,
+    south,
     forcing,
     partial,
     pair_in,
@@ -137,6 +139,11 @@
                 for level in range(levels):
                     yield (index * 2 + parity) * levels + level, array, parity, level
 
+    def turn_south(first, last):
+        for k in range(first, last):
+            odd = north[at(k, 1, 0, 0) : at(k, 1, 0, 0) + SUBLANES, :]
+            south[k * SUBLANES : (k + 1) * SUBLANES, :] = pltpu.roll(odd, 1, 1)
+
     def send_edges(kind, arrays):
         stride = len(arrays) * 2 * levels
         for q, array, parity, level in slots(arrays):
@@ -176,7 +183,11 @@
                 kind, 1, pl.ds(q, STEPS, stride=stride), :
             ]
 
-    def step(first, last, span, load, store):
+    def sweep(section, first, last, load, store):
+        if section > 1:
+            load = functools.partial(load_work, section - 2)
+        if section < STEPS:
+            store = functools.partial(store_work, section - 1)
         behind = []
         current = []
         for member in range(members):
@@ -184,42 +195,44 @@
             old, here = pair[:rows], pair[rows:]
             behind.append(east[(first - 1) * rows : first * rows, :] * (here - old))
             current.append(here)
-        for k in range(first, last, span):
-            lanes = slice(k * rows, (k + span) * rows)
-            coef_east = east[lanes, :]
-            coef_north = north[lanes, :].reshape(span, 2, SUBLANES, LANES)
+        for k in range(first, last, SPAN):
+            span = min(SPAN, last - k)
+            coef_east = east[k * rows : (k + span) * rows, :]
+            coef_north = north[k * rows : (k + span) * rows, :].reshape(span, 2, SUBLANES, LANES)
+            coef_south = south[k * SUBLANES : (k + span) * SUBLANES, :].reshape(span, SUBLANES, LANES)
             results = []
             for member in range(members):
                 after = load(member, k + 1, span)
-                here = jnp.concatenate([current[member], after[: (span - 1) * rows]], axis=0)
-                flux = coef_east * (after - here)
-                west = jnp.concatenate([behind[member], flux[: (span - 1) * rows]], axis=0)
+                here, west = current[member], behind[member]
+                flux = coef_east * (after - here if span == 1 else after - jnp.concatenate([here, after[:-rows]]))
+                if span > 1:
+                    here = jnp.concatenate([here, after[:-rows]])
+                    west = jnp.concatenate([west, flux[:-rows]])
                 pairs = here.reshape(span, 2, SUBLANES, LANES)
                 even, odd = pairs[:, 0], pairs[:, 1]
-                even_flux = coef_north[:, 0] * (odd - even)
-                odd_flux = coef_north[:, 1] * (pltpu.roll(even, LANES - 1, 2) - odd)
-                change = jnp.stack([even_flux - pltpu.roll(odd_flux, 1, 2), odd_flux - even_flux], axis=1)
+                middle = coef_north[:, 0] * (odd - even)
+                upper = coef_north[:, 1] * (pltpu.roll(even, LANES - 1, 2) - odd)
+                lower = coef_south * (even - pltpu.roll(odd, 1, 2))
+                change = jnp.stack([middle - lower, upper - middle], axis=1)
                 results.append(here + (flux - west) + change.reshape(span * rows, LANES))
-                current[member] = after[(span - 1) * rows :]
-                behind[member] = flux[(span - 1) * rows :]
+                current[member] = after[-rows:]
+                behind[member] = flux[-rows:]
             store(k, span, results)
 
-    def load_work(member, k, count):
-        return work[member, k * rows : (k + count) * rows, :]
-
-    def store_work(k, count, results):
+    def load_work(index, member, k, count):
+        return work[index, member, k * rows : (k + count) * rows, :]
+
+    def store_work(index, k, count, results):
         for member in range(members):
-            work[member, k * rows : (k + count) * rows, :] = results[member]
-
-    def diffuse(load, store):
-        step(1, wide - 1, 6, load, store_work)
-
-        def middle(section, unused):
-            step(2, wide - 2, 4, load_work, store_work)
-            return unused
-
-        lax.fori_loop(0, STEPS - 2, middle, 0)
-        step(STEPS, STEPS + cols, 4, load_work, store)
+            work[index, member, k * rows : (k + count) * rows, :] = results[member]
+
+    def diffuse(load, store, arrive):
+        for section in range(1, STEPS + 1):
+            sweep(section, STEPS + section, STEPS + cols - section, load, store)
+        arrive()
+        for section in range(1, STEPS + 1):
+            sweep(section, section, STEPS + section, load, store)
+            sweep(section, STEPS + cols - section, wide - section, load, store)
 
     def load_controls(member, k, count):
         return ctl[member, k * rows : (k + count) * rows, :]
@@ -366,10 +379,20 @@
     send_edges(ENSEMBLE, members_of)
     start_edges(ENSEMBLE)
 
-    seams(controls)
-    seams([east, north])
-    take_edges(0, controls)
-    take_edges(KAPPAS, [east, north])
+    turn_south(STEPS, STEPS + cols)
+
+    def arrive_controls(kind):
+        seams(controls)
+        if kind == 0:
+            seams([east, north])
+            take_edges(KAPPAS, [east, north])
+            turn_south(0, STEPS)
+            turn_south(STEPS + cols, wide)
+        take_edges(kind, controls)
+
+    def arrive_forcing(kind):
+        seams([forcing])
+        take_edges(kind, [forcing])
 
     for iteration in range(ITERS):
         if iteration > 0:
@@ -379,7 +402,7 @@
                 all_copy(hop, mine).wait_send()
             for hop in range(pairs):
                 pass_copy(hop, core).wait_send()
-        diffuse(load_controls, store_sum)
+        diffuse(load_controls, store_sum, functools.partial(arrive_controls, iteration))
         pair_copy().start()
 
         pair_copy().wait_recv()
@@ -422,7 +445,6 @@
             pass_copy(hop, 1 - core).wait_recv()
         send_edges(FORCING + iteration, [forcing])
         start_edges(FORCING + iteration)
-        seams([forcing])
 
         if iteration == ITERS - 1:
             plane[...] = jnp.zeros_like(plane)
@@ -445,14 +467,10 @@
                 inc_copy(off, me).start()
             inc_in[tile(chunk_of(me), packed), :] = inc_out[tile(me, packed), :]
 
-        take_edges(FORCING + iteration, [forcing])
-
-        diffuse(load_forced, store_update)
+        diffuse(load_forced, store_update, functools.partial(arrive_forcing, FORCING + iteration))
         if iteration < ITERS - 1:
             send_edges(iteration + 1, controls)
             start_edges(iteration + 1)
-            seams(controls)
-            take_edges(iteration + 1, controls)
 
     for member in range(members):
         for level in range(levels):
@@ -518,9 +536,10 @@
         scratch_shapes=[
             buffer(members, wide),
             buffer(members, wide),
-            buffer(members, wide),
+            buffer(STEPS - 1, members, wide),
             buffer(wide),
             buffer(wide),
+            buffer(wide // 2),
             buffer(wide),
             buffer(cols * rows),
             buffer(n_mem // 2 * own_cols * rows),

time: 58.9 us -> 52.8 us (0.90)
  Pallas kernels: 55.3 us -> 49.5 us
    pallas_call x1, Pallas kernels: 55.3 us -> 49.5 us  [body(): pl.pallas_call(functools.partial(kernel, n_mem, n_lon), out_shape=(jax.Sh...]
where the time goes in v3:
time: 52.8 us; the launch traced here: 52.7 us
  Pallas kernels  49.5 us (94%)
  local copies, waits for them, and re-layouts  2.48 us (5%)
  between operations  0.65 us (1%)
    pallas_call x1, Pallas kernels, body(): pl.pallas_call(functools.partial(kernel, n_mem, n_lon), out_shape=(jax.Sh...  49.5 us
    unnamed x4, local copies, waits for them, and re-layouts  2.48 us

profile of v3, /device:TPU:0, one launch (start us, length us, event | category | flops | bytes accessed | tf_op | source)
XLA Modules:
  0.0 52.7 jit_solution(16664812703771044016)
XLA Ops:
  0.6 49.5 %shard_map.95 = (f32[2,2,256,128]{3,2,1,0:T(8,128)}, f32[2,16,128]{2,1,0:T(8,128)}) custom-call(bf16[2,2,256,128]{3,2,1,0:T(8,128)(2,1)} %ens_hbm.1, f32[2,2,256,128]{3,2,1,0:T(8,128)} %start_hbm.1, f32[2,256,128]{2,1,0:T(8,128)} %east_hbm.1, f32[2,256,128]{2,1,0:T(8,128)} %north_hbm.1, f32[2,16,128]{2,1,0:T(8,128)} %innov_hbm.1, s32[2,16,128]{2,1,0:T(8,128)} %mask_hbm.1, ...), custom_call_target="tpu_custom_call" | custom-call | flops 56623104 | bytes 2097152 | tf_op jit(solution)/shard_map/pallas_call | solution.py:528
  50.2 0.0 copy-start
  50.2 1.9 %copy.12 = f32[2,2,256,128]{3,2,1,0:T(8,128)} copy(f32[2,2,256,128]{3,2,1,0:T(8,128)} %get-tuple-element.4) | data formatting | bytes 1048576
  52.1 0.0 copy-done
  52.1 0.6 %copy.13 = f32[2,16,128]{2,1,0:T(8,128)} copy(f32[2,16,128]{2,1,0:T(8,128)S(1)} %copy-done) | data formatting | bytes 32768
Async XLA Ops:
  50.2 1.9 %copy-start = (f32[2,16,128]{2,1,0:T(8,128)S(1)}, f32[2,16,128]{2,1,0:T(8,128)}, u32[]{:S(2)}) copy-start(f32[2,16,128]{2,1,0:T(8,128)} %get-tuple-element.5) | copy-start | bytes 49156

commit v4 on v3

--- a/solution.py
+++ b/solution.py
@@ -282,14 +282,38 @@
     def sender(off):
         return lax.rem(me + n_mem - off, n_mem)
 
-    def pair_copy():
-        half = pairs * chunk
-        return send(partial.at[tile(1 - core, half)], pair_in, pair_send.at[0], pair_recv.at[0], sibling)
+    strip_chunks = STEPS // own_cols
+    strip_rows = strip_chunks * chunk
+    inner_rows = pairs * chunk - strip_rows
+
+    def pair_copy(piece, half):
+        if piece == 0:
+            source, target, size = strip_rows + half * inner_rows, strip_rows * (1 - half), inner_rows
+        else:
+            source, target, size = half * (pairs * chunk + inner_rows), half * inner_rows, strip_rows
+        return send(
+            partial.at[pl.ds(pl.multiple_of(source, SUBLANES), size)],
+            pair_in.at[pl.ds(pl.multiple_of(target, SUBLANES), size)],
+            pair_send.at[piece],
+            pair_recv.at[piece],
+            sibling,
+        )
 
     def sum_copy(hop):
         to = lax.rem(group + hop, pairs)
         source = partial.at[tile(core * pairs + to, chunk)]
         return send(source, landing.at[hop], sum_send.at[hop], sum_recv.at[hop], to * 2 + core)
+
+    def start_sums(piece):
+        pair_copy(piece, core).wait_recv()
+        for place in range(strip_chunks, pairs) if piece == 0 else range(strip_chunks):
+            to = place + core * (pairs - 1 - 2 * place)
+            hop = lax.rem(to - group + pairs, pairs)
+
+            @pl.when(hop != 0)
+            def _():
+                partial[tile(core * pairs + to, chunk), :] += pair_in[tile(to, chunk), :]
+                sum_copy(hop).start()
 
     def block_of(index):
         return pl.ds(pl.multiple_of(STEPS * rows + index * chunk, rows), chunk)
@@ -382,7 +406,10 @@
     turn_south(STEPS, STEPS + cols)
 
     def arrive_controls(kind):
+        pair_copy(0, 1 - core).start()
         seams(controls)
+        if kind > 0:
+            start_sums(0)
         if kind == 0:
             seams([east, north])
             take_edges(KAPPAS, [east, north])
@@ -396,20 +423,18 @@
 
     for iteration in range(ITERS):
         if iteration > 0:
-            pair_copy().wait_send()
+            for piece in range(2):
+                pair_copy(piece, 1 - core).wait_send()
             for hop in hops:
                 sum_copy(hop).wait_send()
                 all_copy(hop, mine).wait_send()
             for hop in range(pairs):
                 pass_copy(hop, core).wait_send()
         diffuse(load_controls, store_sum, functools.partial(arrive_controls, iteration))
-        pair_copy().start()
-
-        pair_copy().wait_recv()
-        for hop in hops:
-            to = lax.rem(group + hop, pairs)
-            partial[tile(core * pairs + to, chunk), :] += pair_in[tile(to, chunk), :]
-            sum_copy(hop).start()
+        pair_copy(1, 1 - core).start()
+        if iteration == 0:
+            start_sums(0)
+        start_sums(1)
         total = partial[tile(mine, chunk), :] + pair_in[tile(group, chunk), :]
         if iteration == 0:
             seams(members_of)
@@ -438,14 +463,6 @@
             all_copy(hop, mine).start()
         pass_copy(0, core).start()
 
-        for hop in hops:
-            all_copy(hop, core * pairs + lax.rem(group + pairs - hop, pairs)).wait_recv()
-            pass_copy(hop, core).start()
-        for hop in range(pairs):
-            pass_copy(hop, 1 - core).wait_recv()
-        send_edges(FORCING + iteration, [forcing])
-        start_edges(FORCING + iteration)
-
         if iteration == ITERS - 1:
             plane[...] = jnp.zeros_like(plane)
             for parity in range(2):
@@ -463,6 +480,16 @@
                     )
                     block = jnp.where(lane // half_block == c, moved, block)
                 inc_out[target * packed : (target + 1) * packed, :] = block
+
+        for hop in hops:
+            all_copy(hop, core * pairs + lax.rem(group + pairs - hop, pairs)).wait_recv()
+            pass_copy(hop, core).start()
+        for hop in range(pairs):
+            pass_copy(hop, 1 - core).wait_recv()
+        send_edges(FORCING + iteration, [forcing])
+        start_edges(FORCING + iteration)
+
+        if iteration == ITERS - 1:
             for off in offsets:
                 inc_copy(off, me).start()
             inc_in[tile(chunk_of(me), packed), :] = inc_out[tile(me, packed), :]
@@ -493,7 +520,8 @@
             start = (parity * levels + level) * half_block
             increment_ref[level, pl.ds(parity, half_block, stride=2), :] = turned[start : start + half_block]
 
-    pair_copy().wait_send()
+    for piece in range(2):
+        pair_copy(piece, 1 - core).wait_send()
     for hop in hops:
         sum_copy(hop).wait_send()
         all_copy(hop, mine).wait_send()

time: 52.8 us -> 50 us (0.947)
  Pallas kernels: 49.5 us -> 46.7 us
    pallas_call x1, Pallas kernels: 49.5 us -> 46.7 us  [body(): pl.pallas_call(functools.partial(kernel, n_mem, n_lon), out_shape=(jax.Sh...]
where the time goes in v4:
time: 50 us; the launch traced here: 49.8 us
  Pallas kernels  46.7 us (93%)
  local copies, waits for them, and re-layouts  2.48 us (5%)
  between operations  0.65 us (1%)
    pallas_call x1, Pallas kernels, body(): pl.pallas_call(functools.partial(kernel, n_mem, n_lon), out_shape=(jax.Sh...  46.7 us
    unnamed x4, local copies, waits for them, and re-layouts  2.48 us

profile of v4, /device:TPU:0, one launch (start us, length us, event | category | flops | bytes accessed | tf_op | source)
XLA Modules:
  0.0 49.8 jit_solution(12288520474715654949)
XLA Ops:
  0.6 46.7 %shard_map.95 = (f32[2,2,256,128]{3,2,1,0:T(8,128)}, f32[2,16,128]{2,1,0:T(8,128)}) custom-call(bf16[2,2,256,128]{3,2,1,0:T(8,128)(2,1)} %ens_hbm.1, f32[2,2,256,128]{3,2,1,0:T(8,128)} %start_hbm.1, f32[2,256,128]{2,1,0:T(8,128)} %east_hbm.1, f32[2,256,128]{2,1,0:T(8,128)} %north_hbm.1, f32[2,16,128]{2,1,0:T(8,128)} %innov_hbm.1, s32[2,16,128]{2,1,0:T(8,128)} %mask_hbm.1, ...), custom_call_target="tpu_custom_call" | custom-call | flops 56623104 | bytes 2097152 | tf_op jit(solution)/shard_map/pallas_call | solution.py:556
  47.4 0.0 copy-start
  47.4 1.9 %copy.12 = f32[2,2,256,128]{3,2,1,0:T(8,128)} copy(f32[2,2,256,128]{3,2,1,0:T(8,128)} %get-tuple-element.4) | data formatting | bytes 1048576
  49.2 0.0 copy-done
  49.2 0.6 %copy.13 = f32[2,16,128]{2,1,0:T(8,128)} copy(f32[2,16,128]{2,1,0:T(8,128)S(1)} %copy-done) | data formatting | bytes 32768
Async XLA Ops:
  47.4 1.9 %copy-start = (f32[2,16,128]{2,1,0:T(8,128)S(1)}, f32[2,16,128]{2,1,0:T(8,128)}, u32[]{:S(2)}) copy-start(f32[2,16,128]{2,1,0:T(8,128)} %get-tuple-element.5) | copy-start | bytes 49156

commit v5 on v4

--- a/solution.py
+++ b/solution.py
@@ -87,6 +87,8 @@
     packed = obs_out.shape[0] // n_mem
     scale = float(n_mem * members) ** (-0.5)
     me = lax.axis_index("mem")
+    core = lax.rem(me, 2)
+    sibling = me + 1 - 2 * core
     my_lon = lax.axis_index("lon")
     right = lax.rem(my_lon + 1, n_lon)
     left = lax.rem(my_lon + n_lon - 1, n_lon)
@@ -114,6 +116,7 @@
         pl.semaphore_signal(barrier, inc=1, device_id={"mem": lax.rem(me + off, n_mem)}, device_id_type=MESH)
     for side in (left, right):
         pl.semaphore_signal(barrier, inc=1, device_id={"lon": side}, device_id_type=MESH)
+        pl.semaphore_signal(barrier, inc=1, device_id={"mem": sibling, "lon": side}, device_id_type=MESH)
 
     def at(k, parity, part, level):
         return k * rows + parity * SUBLANES + part * levels + level
@@ -133,6 +136,16 @@
             device_id_type=MESH,
         )
 
+    def forcing_copy(kind, way, index, to):
+        return pltpu.make_async_remote_copy(
+            src_ref=edge_out.at[kind, way],
+            dst_ref=edge_in.at[kind, way],
+            send_sem=edge_send.at[kind, index],
+            recv_sem=edge_recv.at[kind, way],
+            device_id={"mem": to, "lon": (right, left)[way]},
+            device_id_type=MESH,
+        )
+
     def slots(arrays):
         for index, array in enumerate(arrays):
             for parity in range(2):
@@ -144,15 +157,12 @@
             odd = north[at(k, 1, 0, 0) : at(k, 1, 0, 0) + SUBLANES, :]
             south[k * SUBLANES : (k + 1) * SUBLANES, :] = pltpu.roll(odd, 1, 1)
 
-    def send_edges(kind, arrays):
+    def send_edges(kind, arrays, ways=(0, 1)):
         stride = len(arrays) * 2 * levels
         for q, array, parity, level in slots(arrays):
-            edge_out[kind, 0, pl.ds(q, STEPS, stride=stride), :] = array[
-                pl.ds(at(cols, parity, parts - 1, level), STEPS, stride=rows), :
-            ]
-            edge_out[kind, 1, pl.ds(q, STEPS, stride=stride), :] = array[
-                pl.ds(at(STEPS, parity, 0, level), STEPS, stride=rows), :
-            ]
+            for way in ways:
+                first = (at(cols, parity, parts - 1, level), at(STEPS, parity, 0, level))[way]
+                edge_out[kind, way, pl.ds(q, STEPS, stride=stride), :] = array[pl.ds(first, STEPS, stride=rows), :]
 
     def start_edges(kind):
         for way in range(2):
@@ -254,6 +264,11 @@
             before = ctl[member, span, :]
             ctl[member, span, :] = before - STEP_SIZE * (before + results[member])
 
+    def store_last(k, count, results):
+        span = slice(k * rows, (k + count) * rows)
+        for member in range(members):
+            ctl[member, span, :] = ctl[member, span, :] - results[member]
+
     def tile(index, size):
         return pl.ds(pl.multiple_of(index * size, size), size)
 
@@ -268,9 +283,7 @@
         )
 
     pairs = n_mem // 2
-    core = lax.rem(me, 2)
     group = lax.div(me, 2)
-    sibling = me + 1 - 2 * core
     offsets = range(1, n_mem)
     hops = range(1, pairs)
 
@@ -346,7 +359,7 @@
                 )
     controls = [ctl.at[member] for member in range(members)]
     send_edges(0, controls)
-    pl.semaphore_wait(barrier, n_mem - 1 + 2)
+    pl.semaphore_wait(barrier, n_mem - 1 + 4)
     start_edges(0)
 
     fetches[1].wait()
@@ -484,17 +497,24 @@
         for hop in hops:
             all_copy(hop, core * pairs + lax.rem(group + pairs - hop, pairs)).wait_recv()
             pass_copy(hop, core).start()
+        for way in range(2):
+
+            @pl.when(core == 1 - way)
+            def _():
+                send_edges(FORCING + iteration, [forcing], (way,))
+                forcing_copy(FORCING + iteration, way, 0, me).start()
+                forcing_copy(FORCING + iteration, way, 1, sibling).start()
+
         for hop in range(pairs):
             pass_copy(hop, 1 - core).wait_recv()
-        send_edges(FORCING + iteration, [forcing])
-        start_edges(FORCING + iteration)
 
         if iteration == ITERS - 1:
             for off in offsets:
                 inc_copy(off, me).start()
             inc_in[tile(chunk_of(me), packed), :] = inc_out[tile(me, packed), :]
 
-        diffuse(load_forced, store_update, functools.partial(arrive_forcing, FORCING + iteration))
+        store = store_last if iteration == ITERS - 1 else store_update
+        diffuse(load_forced, store, functools.partial(arrive_forcing, FORCING + iteration))
         if iteration < ITERS - 1:
             send_edges(iteration + 1, controls)
             start_edges(iteration + 1)
@@ -553,7 +573,7 @@
     pairs = [pltpu.SemaphoreType.DMA((kinds, 2))] * 2 + [pltpu.SemaphoreType.DMA((n_mem,))] * 12
     vmem = pl.BlockSpec(memory_space=pltpu.VMEM)
     flops = 4 * ITERS * STEPS * members * levels * lat * lon * 9
-    return pl.pallas_call(
+    difference, increment = pl.pallas_call(
         functools.partial(kernel, n_mem, n_lon),
         out_shape=(
             jax.ShapeDtypeStruct(controls_start.shape, jnp.float32),
@@ -596,6 +616,7 @@
         ),
         cost_estimate=pl.CostEstimate(flops=flops, bytes_accessed=2 * 1024 * 1024, transcendentals=0),
     )(ensemble, controls_start, kappa_east, kappa_north, innovation, obs_mask, gauge_index, gauge_precision)
+    return (1.0 - STEP_SIZE) * difference, increment
 
 
 def solution(mesh):

time: 50 us -> 48.9 us (0.978)
  other arithmetic: 0 us -> 1.88 us
  local copies, waits for them, and re-layouts: 2.48 us -> 0.61 us
  Pallas kernels: 46.7 us -> 45.6 us
    mul x0 -> x1, other arithmetic: none -> 1.88 us  [body(): return ((1.0 - STEP_SIZE) * difference, increment)]
    unnamed x4 -> x3, local copies, waits for them, and re-layouts: 2.48 us -> 0.61 us
    pallas_call x1, Pallas kernels: 46.7 us -> 45.6 us  [body(): pl.pallas_call(functools.partial(kernel, n_mem, n_lon), out_shape=(jax.Sh...]
where the time goes in v5:
time: 48.9 us; the launch traced here: 48.7 us
  Pallas kernels  45.6 us (93%)
  other arithmetic  1.88 us (4%)
  between operations  0.65 us (1%)
  local copies, waits for them, and re-layouts  0.61 us (1%)
    pallas_call x1, Pallas kernels, body(): pl.pallas_call(functools.partial(kernel, n_mem, n_lon), out_shape=(jax.Sh...  45.6 us
    mul x1, other arithmetic, body(): return ((1.0 - STEP_SIZE) * difference, increment)  1.88 us

profile of v5, /device:TPU:0, one launch (start us, length us, event | category | flops | bytes accessed | tf_op | source)
XLA Modules:
  0.0 48.7 jit_solution(96776913073373428)
XLA Ops:
  0.6 45.6 %shard_map.95 = (f32[2,2,256,128]{3,2,1,0:T(8,128)}, f32[2,16,128]{2,1,0:T(8,128)}) custom-call(bf16[2,2,256,128]{3,2,1,0:T(8,128)(2,1)} %ens_hbm.1, f32[2,2,256,128]{3,2,1,0:T(8,128)} %start_hbm.1, f32[2,256,128]{2,1,0:T(8,128)} %east_hbm.1, f32[2,256,128]{2,1,0:T(8,128)} %north_hbm.1, f32[2,16,128]{2,1,0:T(8,128)} %innov_hbm.1, s32[2,16,128]{2,1,0:T(8,128)} %mask_hbm.1, ...), custom_call_target="tpu_custom_call" | custom-call | flops 56623104 | bytes 2097152 | tf_op jit(solution)/shard_map/pallas_call | solution.py:576
  46.2 0.0 copy-start
  46.3 1.9 %broadcast_multiply_fusion = f32[2,2,256,128]{3,2,1,0:T(8,128)} fusion(f32[2,2,256,128]{3,2,1,0:T(8,128)} %get-tuple-element.4), kind=kLoop, calls=%fused_computation | loop fusion | flops 131072 | bytes 1048576 | tf_op jit(solution)/shard_map/mul | solution.py:619
  48.1 0.0 copy-done
  48.1 0.6 %copy.11 = f32[2,16,128]{2,1,0:T(8,128)} copy(f32[2,16,128]{2,1,0:T(8,128)S(1)} %copy-done) | data formatting | bytes 32768
Async XLA Ops:
  46.2 1.9 %copy-start = (f32[2,16,128]{2,1,0:T(8,128)S(1)}, f32[2,16,128]{2,1,0:T(8,128)}, u32[]{:S(2)}) copy-start(f32[2,16,128]{2,1,0:T(8,128)} %get-tuple-element.9) | copy-start | bytes 49156
